TPU v7x, 32 devices: a whole 2x2x4 slice. The times are simulated.
32 devices in a mesh: grp: 4 (over y, x), dev: 8 (over z, core).
Axes of the slice: x: 2, y: 2, z: 4, core: 2. Of those that a mesh axis runs over, the one named last changes fastest.
Arguments:
- phi: bfloat16 [256, 8192], P(('grp', 'dev')), may hold values from -6 to 6
- conf: float32 [256], P(('grp', 'dev')), may hold values from 0.5 to 8
- shift_energy: float32 [256], P(('grp', 'dev')), may hold values from 0.5 to 3
- kern: float32 [256, 80], P(('grp', 'dev')), may hold values from -2 to 2
- margins: int32 [256, 8], P(('grp', 'dev')), may hold values from 0 to 255, as said below
- offsets: int32 [256, 3], replicated, may hold values from 0 to 8
Outputs:
- gradient: float32 [256, 8192], P(('grp', 'dev'))
- updated: bfloat16 [256, 8192], P(('grp', 'dev'))
Inputs may be any that keep to these rules, and one draw needn't show every extreme that they name: `margins`: the 8 entries of a row are distinct; at most two of them lie outside the row's group, and those belong to the function's device index in the group just below or just above.
All inputs are finite; a program needn't handle non-finite values.
Results may differ from a plain program's by a relative error of at most 0.0039.
Values may be sent and summed in bfloat16 or wider, within the bound.
A program may use at most 64 MiB of HBM per device.

v0:
```python
import jax
import jax.numpy as jnp
from jax import lax
from jax.sharding import PartitionSpec as P

BX = 16
BY = 16
BZ = 32


def with_halo(cells, sides, width):
    for axis, dim in sides:
        count = lax.axis_size(axis)
        ends = count - 1
        head = lax.slice_in_dim(cells, 0, width, axis=dim)
        tail = lax.slice_in_dim(cells, cells.shape[dim] - width, cells.shape[dim], axis=dim)
        cells = jnp.concatenate(
            [
                lax.ppermute(tail, axis, [(i, (i + 1) % count) for i in range(ends)]),
                cells,
                lax.ppermute(head, axis, [((i + 1) % count, i) for i in range(ends)]),
            ],
            axis=dim,
        )
    return cells


def apply_ham(phi, conf, shift_energy):
    count = phi.shape[0]
    field = phi.astype(jnp.float32).reshape(count, BX, BY, BZ)
    padded = jnp.pad(field, ((0, 0), (1, 1), (1, 1), (1, 1)))
    lap = padded[:, 2:, 1:-1, 1:-1] + padded[:, :-2, 1:-1, 1:-1]
    lap = lap + padded[:, 1:-1, 2:, 1:-1] + padded[:, 1:-1, :-2, 1:-1]
    lap = lap + padded[:, 1:-1, 1:-1, 2:] + padded[:, 1:-1, 1:-1, :-2] - 6.0 * field
    coord_x = (jnp.arange(BX, dtype=jnp.float32) - (BX - 1) / 2.0) / BX
    coord_y = (jnp.arange(BY, dtype=jnp.float32) - (BY - 1) / 2.0) / BY
    coord_z = (jnp.arange(BZ, dtype=jnp.float32) - (BZ - 1) / 2.0) / BZ
    radius = coord_x[:, None, None] ** 2 + coord_y[None, :, None] ** 2 + coord_z[None, None, :] ** 2
    value = (
        -0.5 * lap
        + conf[:, None, None, None] * radius[None] * field
        - shift_energy[:, None, None, None] * field
    )
    return value.reshape(count, BX * BY * BZ).astype(jnp.bfloat16)


def onehot(size, delta):
    steps = jnp.arange(size, dtype=jnp.int32)
    return (
        steps[None, None, None, :] == steps[None, None, :, None] + delta[:, :, None, None]
    ).astype(jnp.bfloat16)


def pick_rows(carry, piece, position, wanted):
    rows = piece.shape[0]
    inside = wanted & (position >= 0) & (position < rows)
    taken = piece[jnp.clip(position, 0, rows - 1)]
    return jnp.where(inside[:, :, None], taken, carry)


def on_device(phi, conf, shift_energy, kern, margins, offsets):
    fn_rows = phi.shape[0]
    width = kern.shape[1]
    per_group = width - 2 * fn_rows
    group_idx = lax.axis_index("grp")
    device_idx = lax.axis_index("dev")
    local = jnp.arange(fn_rows, dtype=jnp.int32)
    own_ids = (group_idx * lax.axis_size("dev") + device_idx) * fn_rows + local
    own_off = offsets[own_ids]
    columns = jnp.arange(width, dtype=jnp.int32)
    u_own = apply_ham(phi, conf, shift_energy)
    group_b = margins // per_group
    same = group_b == group_idx
    lower = group_b == group_idx - 1
    upper = group_b == group_idx + 1
    col = jnp.where(
        same,
        margins - group_b * per_group,
        jnp.where(lower, per_group + margins % fn_rows, per_group + fn_rows + margins % fn_rows),
    )
    weight = jnp.sum(
        kern[:, None, :] * (columns[None, None, :] == col[:, :, None]).astype(jnp.float32), axis=2
    )
    start_rows = jnp.zeros((fn_rows, margins.shape[1], u_own.shape[1]), jnp.bfloat16)
    window = with_halo(u_own, (("grp", 0),), fn_rows)
    segment = group_b - group_idx + 1
    within = margins % per_group
    position = within // fn_rows * (3 * fn_rows) + segment * fn_rows + within % fn_rows
    everywhere = same | lower | upper
    chosen = pick_rows(
        start_rows, lax.all_gather(window, "dev", axis=0, tiled=True), position, everywhere
    )
    delta = own_off[:, None, :] - offsets[margins]
    shaped = chosen.reshape(fn_rows, margins.shape[1], BX, BY, BZ)
    moved = jnp.einsum(
        "apxX,apXyz->apxyz", onehot(BX, delta[:, :, 0]), shaped, preferred_element_type=jnp.float32
    ).astype(jnp.bfloat16)
    moved = jnp.einsum(
        "apyY,apxYz->apxyz", onehot(BY, delta[:, :, 1]), moved, preferred_element_type=jnp.float32
    ).astype(jnp.bfloat16)
    moved = jnp.einsum(
        "apzZ,apxyZ->apxyz", onehot(BZ, delta[:, :, 2]), moved, preferred_element_type=jnp.float32
    )
    gradient = jnp.sum(weight[:, :, None, None, None] * moved, axis=1).reshape(fn_rows, -1)
    stepped = phi.astype(jnp.float32) - 0.5 * gradient
    scale = lax.rsqrt(jnp.mean(stepped * stepped, axis=1, keepdims=True) + 1e-06)
    return (gradient, (stepped * scale).astype(jnp.bfloat16))


def solution(mesh):
    in_specs = (
        P(("grp", "dev"), None),
        P(("grp", "dev")),
        P(("grp", "dev")),
        P(("grp", "dev"), None),
        P(("grp", "dev"), None),
        P(),
    )
    out_specs = (P(("grp", "dev"), None), P(("grp", "dev"), None))
    return jax.shard_map(
        on_device, mesh=mesh, in_specs=in_specs, out_specs=out_specs, check_vma=False
    )
```

profile of v0, /device:TPU:0, one launch (start us, length us, event | category | flops | bytes accessed | tf_op | source)
XLA Modules:
  0.0 90.3 jit_solution(17832510182769811387)
XLA Ops:
  7.2 0.0 all-gather.2.cloned.1.call-start
  7.3 1.2 %reshape.123 = f32[8,16,16,32]{3,2,1,0:T(8,128)S(1)} reshape(bf16[8,8192]{1,0:T(8,128)(2,1)} %param.6) | data formatting | bytes 393216 | tf_op jit(solution)/shard_map/reshape | solution.py:30
  8.5 0.1 broadcast_add_fusion.1
  8.6 0.1 broadcast_add_fusion
  8.7 1.6 %fusion.17 = bf16[8,16,16,32]{3,2,1,0:T(8,128)(2,1)S(1)} fusion(f32[8,16,16,32]{3,2,1,0:T(8,128)S(1)} %reshape.123, f32[8]{0:T(128)} %param.8, f32[16,16,32]{2,1,0:T(8,128)S(1)} %broadcast_add_fusion, f32[8]{0:T(128)} %param.7), kind=kLoop, calls=%fused_computation.27 | loop fusion | flops 917504 | bytes 426048 | tf_op jit(solution)/shard_map/convert_element_type | solution.py:44
  10.3 0.5 convert_element_type.30
  10.8 1.3 %collective-permute-start.1 = (bf16[8,8192]{1,0:T(8,128)(2,1)S(1)}, bf16[8,8192]{1,0:T(8,128)(2,1)S(1)}, u32[]{:S(2)}, u32[]{:S(2)}) collective-permute-start(bf16[8,8192]{1,0:T(8,128)(2,1)S(1)} %convert_element_type.30), channel_id=1, source_target_pairs={{8,0},{16,8},{24,16},{9,1},{17,9},{25,17},{10,2},{18,10},{26,18},{... | collective-permute-start | bytes 393224 | tf_op jit(solution)/shard_map/ppermute | solution.py:21
  12.1 5.5 %collective-permute-start = (bf16[8,8192]{1,0:T(8,128)(2,1)S(1)}, bf16[8,8192]{1,0:T(8,128)(2,1)S(1)}, u32[]{:S(2)}, u32[]{:S(2)}) collective-permute-start(bf16[8,8192]{1,0:T(8,128)(2,1)S(1)} %convert_element_type.30), channel_id=1, source_target_pairs={{0,8},{8,16},{16,24},{1,9},{9,17},{17,25},{2,10},{10,18},{18,26},{... | collective-permute-start | bytes 393224 | tf_op jit(solution)/shard_map/ppermute | solution.py:19
  17.6 1.5 %collective-permute-done.1 = bf16[8,8192]{1,0:T(8,128)(2,1)S(1)} collective-permute-done((bf16[8,8192]{1,0:T(8,128)(2,1)S(1)}, bf16[8,8192]{1,0:T(8,128)(2,1)S(1)}, u32[]{:S(2)}, u32[]{:S(2)}) %collective-permute-start.1) | collective-permute-done | bytes 131104 | tf_op jit(solution)/shard_map/ppermute | solution.py:21
  19.2 1.2 %collective-permute-done = bf16[8,8192]{1,0:T(8,128)(2,1)S(1)} collective-permute-done((bf16[8,8192]{1,0:T(8,128)(2,1)S(1)}, bf16[8,8192]{1,0:T(8,128)(2,1)S(1)}, u32[]{:S(2)}, u32[]{:S(2)}) %collective-permute-start) | collective-permute-done | bytes 131104 | tf_op jit(solution)/shard_map/ppermute | solution.py:19
  20.4 0.8 pad_maximum_fusion
  21.1 0.0 all-gather.2.cloned.1.call-update
  21.2 0.1 reshape.143
  21.3 0.1 copy.12
  21.5 0.1 reshape.135
  21.6 0.6 gather_fusion.1
  22.2 0.1 copy.15
  22.3 0.6 gather_fusion
  22.9 0.1 copy.13
  22.9 0.2 select_reduce_fusion
  23.1 0.1 broadcast_subtract_fusion
  23.2 0.1 iota_add_fusion
  23.2 0.1 iota_add_fusion.1
  23.3 39.6 %all-gather.2.cloned.1.call-done = bf16[192,8192]{1,0:T(8,128)(2,1)} async-done(((bf16[24,8192]{1,0:T(8,128)(2,1)}), bf16[192,8192]{1,0:T(8,128)(2,1)}) %all-gather.2.cloned.1.call-update) | async-done | bytes 3145744 | tf_op jit(solution)/shard_map/all_gather | solution.py:91
  63.0 4.4 %gather_fusion.2 = bf16[64,8192]{1,0:T(8,128)(2,1)S(1)} fusion(bf16[192,8192]{1,0:T(8,128)(2,1)} %all-gather.2.cloned.1.call-done, s32[1024]{0:T(1024)S(1)} %pad_clamp_fusion), kind=kCustom, calls=%fused_computation.2 | custom fusion | bytes 2097408 | tf_op jit(solution)/shard_map/gather | solution.py:57
  67.4 4.4 %gather.14 = bf16[8,8,16,16,32]{4,3,2,1,0:T(8,128)(2,1)} reshape(bf16[64,8192]{1,0:T(8,128)(2,1)S(1)} %gather_fusion.2) | data formatting | bytes 2097152 | tf_op jit(solution)/shard_map/gather | solution.py:57
  71.9 2.5 %broadcast_select_fusion = bf16[8,8,16,16,32]{4,3,2,1,0:T(8,128)(2,1)S(1)} fusion(bf16[8,8,16,16,32]{4,3,2,1,0:T(8,128)(2,1)} %gather.14, pred[8,8]{1,0:T(8,128)(4,1)S(1)} %get-tuple-element.2), kind=kLoop, calls=%fused_computation.11 | loop fusion | flops 524288 | bytes 2097216 | tf_op jit(solution)/shard_map/jit(_where)/select_n | solution.py:58
  74.4 2.8 %fusion.3 = bf16[8,8,16,16,32]{4,2,3,1,0:T(8,128)(2,1)} fusion(bf16[8,8,16,16,32]{4,3,2,1,0:T(8,128)(2,1)S(1)} %broadcast_select_fusion, s32[8,8,16]{2,1,0:T(8,128)S(1)} %get-tuple-element.10), kind=kOutput, calls=%fused_computation.8 | convolution fusion | flops 16793600 | bytes 2101248 | tf_op jit(solution)/shard_map/apxX,apXyz->apxyz/dot_general | solution.py:95
  77.2 4.8 %multiply_reduce_fusion = f32[8,16,16,32]{3,2,1,0:T(8,128)S(1)} fusion(f32[8,8]{1,0:T(8,128)S(1)} %select_reduce_fusion, bf16[8,8,16,16,32]{4,2,3,1,0:T(8,128)(2,1)} %fusion.3, s32[8,8,32]{2,1,0:T(8,128)S(1)} %iota_add_fusion, s32[8,8,16]{2,1,0:T(8,128)S(1)} %get-tuple-element.9), kind=kOutput, calls=%fused_computation.4 | convolution fusion | flops 51920896 | bytes 1323264 | tf_op jit(solution)/shard_map/apzZ,apxyZ->apxyz/dot_general | solution.py:101
  82.0 0.5 reshape.124
  82.5 0.2 multiply_reduce_fusion.1
  82.7 0.7 multiply_convert_fusion
  (21 shorter events, 0.1 us)
Async XLA Ops:
  7.2 14.0 %copy-start.2 = (s32[8,8]{1,0:T(8,128)S(1)}, s32[8,8]{1,0:T(8,128)}, u32[]{:S(2)}) copy-start(s32[8,8]{1,0:T(8,128)} %param.10) | copy-start | bytes 772
  7.2 14.1 %copy-start.3 = (s32[256,3]{0,1:T(4,128)S(1)}, s32[256,3]{0,1:T(4,128)}, u32[]{:S(2)}) copy-start(s32[256,3]{0,1:T(4,128)} %param.11) | copy-start | bytes 9220
  7.2 15.8 %copy-start.4 = (f32[8,80]{1,0:T(8,128)S(1)}, f32[8,80]{1,0:T(8,128)}, u32[]{:S(2)}) copy-start(f32[8,80]{1,0:T(8,128)} %param.9) | copy-start | bytes 7684
  7.2 55.8 %all-gather.2.cloned.1.call-start = ((), (), s32[]{:S(2)}) async-start(), calls=%async_computation | async-start | bytes 3538944 | tf_op jit(solution)/shard_map/all_gather | solution.py:91
  10.8 8.3 %collective-permute-start.1 = (bf16[8,8192]{1,0:T(8,128)(2,1)S(1)}, bf16[8,8192]{1,0:T(8,128)(2,1)S(1)}, u32[]{:S(2)}, u32[]{:S(2)}) collective-permute-start(bf16[8,8192]{1,0:T(8,128)(2,1)S(1)} %convert_element_type.30), channel_id=1, source_target_pairs={{8,0},{16,8},{24,16},{9,1},{17,9},{25,17},{10,2},{18,10},{26,18},{... | collective-permute-start | bytes 393224 | tf_op jit(solution)/shard_map/ppermute | solution.py:21
  12.1 8.2 %collective-permute-start = (bf16[8,8192]{1,0:T(8,128)(2,1)S(1)}, bf16[8,8192]{1,0:T(8,128)(2,1)S(1)}, u32[]{:S(2)}, u32[]{:S(2)}) collective-permute-start(bf16[8,8192]{1,0:T(8,128)(2,1)S(1)} %convert_element_type.30), channel_id=1, source_target_pairs={{0,8},{8,16},{16,24},{1,9},{9,17},{17,25},{2,10},{10,18},{18,26},{... | collective-permute-start | bytes 393224 | tf_op jit(solution)/shard_map/ppermute | solution.py:19
  77.2 5.3 %copy-start.1 = (bf16[8,8192]{1,0:T(8,128)(2,1)S(1)}, bf16[8,8192]{1,0:T(8,128)(2,1)}, u32[]{:S(2)}) copy-start(bf16[8,8192]{1,0:T(8,128)(2,1)} %param.6) | copy-start | bytes 393220
  82.5 1.0 %copy-start = (f32[8,8192]{1,0:T(8,128)}, f32[8,8192]{1,0:T(8,128)S(1)}, u32[]{:S(2)}) copy-start(f32[8,8192]{1,0:T(8,128)S(1)} %reshape.124) | copy-start | bytes 786436
Sparse Core Ops, SparseCore 0:
  21.3 41.6 all-gather.1
where the time goes:
time: 90.6 us; the launch traced here: 90.3 us
  waiting for transfers between devices  42.4 us (47%)
  between operations  14.2 us (16%)
  local copies, waits for them, and re-layouts  12.8 us (14%)
  matrix products  7.61 us (8%)
  starting transfers between devices  6.81 us (8%)
  other arithmetic  6.49 us (7%)
    all_gather x1, waiting for transfers between devices, on_device(): lax.all_gather(window, 'dev', axis=0, tiled=True)  39.6 us
    gather x2, local copies, waits for them, and re-layouts, pick_rows(): taken = piece[jnp.clip(position, 0, rows - 1)]  8.88 us
    ppermute x1, starting transfers between devices, with_halo(): lax.ppermute(tail, axis, [(i, (i + 1) % count) for i in range(ends)])  5.48 us
    dot_general x1, matrix products, on_device(): jnp.einsum('apzZ,apxyZ->apxyz', onehot(BZ, delta[:, :, 2]), moved, prefer...  4.76 us
    dot_general x1, matrix products, on_device(): jnp.einsum('apxX,apXyz->apxyz', onehot(BX, delta[:, :, 0]), shaped, prefe...  2.85 us
    select_n x1, other arithmetic, pick_rows(): return jnp.where(inside[:, :, None], taken, carry)  2.53 us
  transfers between devices with their start and end apart: 3, of which 3 were waited for; matrix products, arithmetic and copies ran while one was open for 2% of the time, Pallas kernels for 0%

commit v1 on v0

v1 whole, which is shorter than its diff:
```python
import functools

import jax
import jax.numpy as jnp
from jax import lax
from jax.experimental import pallas as pl
from jax.experimental.pallas import tpu as pltpu
from jax.sharding import PartitionSpec as P

BX = 16
BY = 16
BZ = 32
LANES = 128
YL = LANES // BZ
YT = BY // YL
ROWS = BX * YT
CHUNKS = 2
MESH = pl.DeviceIdType.MESH


def column(count, scalar_of):
    sub = lax.broadcasted_iota(jnp.int32, (count, LANES), 0)
    out = jnp.full((count, LANES), scalar_of(0))
    for f in range(1, count):
        out = jnp.where(sub == f, scalar_of(f), out)
    return out


def tile_roll(get, put, off_x, off_y, off_z, back):
    shape = off_x.shape
    lane = lax.broadcasted_iota(jnp.int32, shape, 1)
    yl, zz = lane // BZ, lane % BZ
    if back:
        off_x, off_y, off_z = (BX - off_x) % BX, (BY - off_y) % BY, (BZ - off_z) % BZ
    y_lo, y_hi = off_y % YL, off_y // YL
    index = (yl + YL - y_lo) % YL * BZ + (zz + BZ - off_z) % BZ
    carried = yl < y_lo
    y_bits = [(1 << i, (y_hi >> i) % 2 == 1) for i in range(YT.bit_length() - 1)]
    x_bits = [(1 << i, (off_x >> i) % 2 == 1) for i in range(BX.bit_length() - 1)]
    planes = []
    for x in range(BX):
        rows = [jnp.take_along_axis(get(x * YT + t), index, axis=1) for t in range(YT)]
        rows = [jnp.where(carried, rows[(t - 1) % YT], rows[t]) for t in range(YT)]
        for step, on in y_bits:
            rows = [jnp.where(on, rows[(t - step) % YT], rows[t]) for t in range(YT)]
        planes.append(rows)
    for t in range(YT):
        rows = [planes[x][t] for x in range(BX)]
        for step, on in x_bits:
            rows = [jnp.where(on, rows[(x - step) % BX], rows[x]) for x in range(BX)]
        for x in range(BX):
            put(x * YT + t, rows[x])


def kernel(
    groups,
    devs,
    phi_ref,
    conf_ref,
    shift_ref,
    kern_ref,
    margins_ref,
    offsets_ref,
    grad_ref,
    upd_ref,
    gath,
    flat,
    work,
    masks,
    cols,
    send_sem,
    recv_sem,
    halo_send,
):
    fns = phi_ref.shape[0]
    near = margins_ref.shape[1]
    per_group = devs * fns
    nz = devs // 2
    part = fns // CHUNKS
    gi = lax.axis_index("grp")
    me = lax.axis_index("dev")
    core, z = me % 2, me // 2
    sib = me + 1 - 2 * core
    base = (gi * devs + me) * fns

    barrier = pltpu.get_barrier_semaphore()
    links = (
        (z >= 0, (gi, sib)),
        (z > 0, (gi, me - 2)),
        (z < nz - 1, (gi, me + 2)),
        (gi > 0, (gi - 1, me)),
        (gi < groups - 1, (gi + 1, me)),
    )
    for here, target in links:
        @pl.when(here)
        def _():
            pl.semaphore_signal(barrier, inc=1, device_id=target, device_id_type=MESH)

    off = [column(fns, lambda f, c=c: offsets_ref[c, base + f]) for c in range(3)]
    conf = column(fns, lambda f: conf_ref[f])
    shift = column(fns, lambda f: shift_ref[f])
    shape = (fns, LANES)
    lane = lax.broadcasted_iota(jnp.int32, shape, 1)
    yl, zz = lane // BZ, lane % BZ
    zf = (zz.astype(jnp.float32) - (BZ - 1) / 2.0) / BZ
    zero = jnp.zeros(shape, jnp.float32)

    def phi_row(t):
        return phi_ref[:, t * LANES : (t + 1) * LANES].astype(jnp.float32)

    for x in range(BX):
        xf = ((x - (BX - 1) / 2.0) / BX) ** 2
        rows = [phi_row(x * YT + t) for t in range(YT)]
        ups = [pltpu.roll(r, LANES - BZ, 1) for r in rows] + [zero]
        downs = [zero] + [pltpu.roll(r, BZ, 1) for r in rows]
        for t in range(YT):
            field = rows[t]
            lap = phi_row((x + 1) * YT + t) if x < BX - 1 else zero
            if x > 0:
                lap = lap + phi_row((x - 1) * YT + t)
            lap = lap + jnp.where(yl < YL - 1, ups[t], ups[t + 1])
            lap = lap + jnp.where(yl > 0, downs[t + 1], downs[t])
            lap = lap + jnp.where(zz < BZ - 1, pltpu.roll(field, LANES - 1, 1), 0.0)
            lap = lap + jnp.where(zz > 0, pltpu.roll(field, 1, 1), 0.0)
            lap = lap - 6.0 * field
            yf = ((yl + t * YL).astype(jnp.float32) - (BY - 1) / 2.0) / BY
            radius = xf + yf * yf + zf * zf
            work[x * YT + t] = -0.5 * lap + conf * radius * field - shift * field

    def put_flat(t, value):
        flat[pl.ds(t, fns, stride=ROWS), :] = value

    tile_roll(lambda t: work[t], put_flat, off[0], off[1], off[2], False)
    for f in range(fns):
        gath[me * fns + f] = flat[f * ROWS : (f + 1) * ROWS, :].astype(jnp.bfloat16)

    def piece(block, c):
        return gath.at[pl.ds(block * fns + c * part, part)]

    def line(block, c, way, target):
        return pltpu.make_async_remote_copy(
            src_ref=piece(block, c),
            dst_ref=piece(block, c),
            send_sem=send_sem.at[way, block, c],
            recv_sem=recv_sem.at[block, c],
            device_id=(gi, target),
            device_id_type=MESH,
        )

    def halo(up, c):
        return pltpu.make_async_remote_copy(
            src_ref=piece(me, c),
            dst_ref=piece(devs if up else devs + 1, c),
            send_sem=halo_send.at[1 if up else 0, c],
            recv_sem=recv_sem.at[devs if up else devs + 1, c],
            device_id=(gi + 1 if up else gi - 1, me),
            device_id_type=MESH,
        )

    has_left, has_right = z > 0, z < nz - 1
    has_below, has_above = gi > 0, gi < groups - 1

    pl.semaphore_wait(barrier, 1 + sum(jnp.where(h, 1, 0) for h, _ in links[1:]))
    for c in range(CHUNKS):
        @pl.when(has_right)
        def _():
            line(me, c, 0, me + 2).start()

        @pl.when(has_left)
        def _():
            line(me, c, 1, me - 2).start()

        line(me, c, 2, sib).start()
    for c in range(CHUNKS):
        @pl.when(has_above)
        def _():
            halo(True, c).start()

        @pl.when(has_below)
        def _():
            halo(False, c).start()

    row = lax.broadcasted_iota(jnp.int32, (ROWS, LANES), 0)
    lan = lax.broadcasted_iota(jnp.int32, (ROWS, LANES), 1)
    cell = (row // YT, row % YT * YL + lan // BZ, lan % BZ)

    def make_masks(a, carry):
        for k in range(near):
            b = margins_ref[a, k]
            gb = b // per_group
            col = jnp.where(
                gb == gi,
                b - gb * per_group,
                jnp.where(gb == gi - 1, per_group, per_group + fns) + b % fns,
            )
            cols[a * near + k] = col
            keep = None
            for axis in range(3):
                oa, ob = offsets_ref[axis, base + a], offsets_ref[axis, b]
                out = (cell[axis] < jnp.minimum(oa, ob)) | (cell[axis] >= jnp.maximum(oa, ob))
                keep = out if keep is None else keep & out
            masks[a * near + k] = jnp.where(keep, kern_ref[a, col], 0.0)
        return carry

    half = fns // 2
    lax.fori_loop(0, half, make_masks, 0)

    for s in range(1, nz):
        for c in range(CHUNKS):
            @pl.when(z - s >= 0)
            def _():
                block = me - 2 * s
                line(block, c, 0, me + 2).wait_recv()

                @pl.when(has_right)
                def _():
                    line(block, c, 0, me + 2).start()

                line(block, c, 2, sib).start()

            @pl.when(z + s < nz)
            def _():
                block = me + 2 * s
                line(block, c, 1, me - 2).wait_recv()

                @pl.when(has_left)
                def _():
                    line(block, c, 1, me - 2).start()

                line(block, c, 2, sib).start()
        if s == 1:
            lax.fori_loop(half, fns, make_masks, 0)

    for block in range(nz):
        for c in range(CHUNKS):
            line(2 * block + 1 - core, c, 2, sib).wait_recv()
    for c in range(CHUNKS):
        @pl.when(has_below)
        def _():
            halo(True, c).wait_recv()

        @pl.when(has_above)
        def _():
            halo(False, c).wait_recv()

    def add_up(a, carry):
        total = None
        for k in range(near):
            term = masks[a * near + k] * gath[cols[a * near + k]].astype(jnp.float32)
            total = term if total is None else total + term
        flat[pl.ds(pl.multiple_of(a * ROWS, ROWS), ROWS), :] = total
        return carry

    lax.fori_loop(0, fns, add_up, 0)

    squares = [zero]

    def put_grad(t, value):
        grad_ref[:, t * LANES : (t + 1) * LANES] = value
        stepped = phi_row(t) - 0.5 * value
        work[t] = stepped
        squares[0] = squares[0] + stepped * stepped

    tile_roll(lambda t: flat[pl.ds(t, fns, stride=ROWS), :], put_grad, off[0], off[1], off[2], True)
    mean = jnp.sum(squares[0], axis=1, keepdims=True) / (ROWS * LANES)
    scale = lax.rsqrt(mean + 1e-06)
    for t in range(ROWS):
        upd_ref[:, t * LANES : (t + 1) * LANES] = (work[t] * scale).astype(jnp.bfloat16)

    for c in range(CHUNKS):
        for block in range(nz):
            line(2 * block + core, c, 2, sib).wait_send()

            @pl.when(has_right & (block <= z))
            def _():
                line(2 * block + core, c, 0, me + 2).wait_send()

            @pl.when(has_left & (block >= z))
            def _():
                line(2 * block + core, c, 1, me - 2).wait_send()

        @pl.when(has_above)
        def _():
            halo(True, c).wait_send()

        @pl.when(has_below)
        def _():
            halo(False, c).wait_send()


def on_device(groups, devs, phi, conf, shift_energy, kern, margins, offsets):
    fns, cells = phi.shape
    near = margins.shape[1]
    vmem = pl.BlockSpec(memory_space=pltpu.VMEM)
    smem = pl.BlockSpec(memory_space=pltpu.SMEM)
    return pl.pallas_call(
        functools.partial(kernel, groups, devs),
        out_shape=(
            jax.ShapeDtypeStruct((fns, cells), jnp.float32),
            jax.ShapeDtypeStruct((fns, cells), jnp.bfloat16),
        ),
        in_specs=[vmem, smem, smem, smem, smem, smem],
        out_specs=(vmem, vmem),
        scratch_shapes=[
            pltpu.VMEM(((devs + 2) * fns, ROWS, LANES), jnp.bfloat16),
            pltpu.VMEM((fns * ROWS, LANES), jnp.float32),
            pltpu.VMEM((ROWS, fns, LANES), jnp.float32),
            pltpu.VMEM((fns * near, ROWS, LANES), jnp.float32),
            pltpu.SMEM((fns * near,), jnp.int32),
            pltpu.SemaphoreType.DMA((3, devs, CHUNKS)),
            pltpu.SemaphoreType.DMA((devs + 2, CHUNKS)),
            pltpu.SemaphoreType.DMA((2, CHUNKS)),
        ],
        compiler_params=pltpu.CompilerParams(
            collective_id=0, has_side_effects=True, vmem_limit_bytes=32 * 1024 * 1024
        ),
    )(phi, conf, shift_energy, kern, margins, offsets.T)


def solution(mesh):
    in_specs = (
        P(("grp", "dev"), None),
        P(("grp", "dev")),
        P(("grp", "dev")),
        P(("grp", "dev"), None),
        P(("grp", "dev"), None),
        P(),
    )
    out_specs = (P(("grp", "dev"), None), P(("grp", "dev"), None))
    return jax.shard_map(
        functools.partial(on_device, mesh.shape["grp"], mesh.shape["dev"]),
        mesh=mesh,
        in_specs=in_specs,
        out_specs=out_specs,
        check_vma=False,
    )
```

time: 90.6 us -> 24.2 us (0.27)
  the two profiles are of different devices: /device:TPU:0 before, /device:TPU:1 now
where the time goes in v1:
time: 24.2 us; the launch traced here: 24 us
  Pallas kernels  18.3 us (76%)
  local copies, waits for them, and re-layouts  4.98 us (21%)
  between operations  0.66 us (3%)
    pallas_call x1, Pallas kernels, on_device(): pl.pallas_call(functools.partial(kernel, groups, devs), out_shape=(jax.Sh...  18.3 us
    unnamed x14, local copies, waits for them, and re-layouts  4.98 us

profile of v1, /device:TPU:1, one launch (start us, length us, event | category | flops | bytes accessed | tf_op | source)
XLA Modules:
  0.0 24.0 jit_solution(7015494207647113611)
XLA Ops:
  0.6 0.0 copy-start.5
  0.6 0.0 copy-start.4
  0.7 0.6 %copy-done.5 = f32[8]{0:T(128)S(1)} copy-done((f32[8]{0:T(128)S(1)}, f32[8]{0:T(128)}, u32[]{:S(2)}) %copy-start.5) | copy-done | bytes 56
  1.3 0.0 copy-done.4
  1.3 0.0 copy-start
  1.3 0.9 %copy-done = bf16[8,8192]{1,0:T(8,128)(2,1)S(1)} copy-done((bf16[8,8192]{1,0:T(8,128)(2,1)S(1)}, bf16[8,8192]{1,0:T(8,128)(2,1)}, u32[]{:S(2)}) %copy-start) | copy-done | bytes 131096
  2.2 0.0 copy-start.1
  2.2 0.7 %copy-done.1 = f32[8,80]{1,0:T(8,128)S(1)} copy-done((f32[8,80]{1,0:T(8,128)S(1)}, f32[8,80]{1,0:T(8,128)}, u32[]{:S(2)}) %copy-start.1) | copy-done | bytes 2584
  2.9 0.0 copy-start.2
  2.9 0.7 %copy-done.2 = s32[8,8]{1,0:T(8,128)S(1)} copy-done((s32[8,8]{1,0:T(8,128)S(1)}, s32[8,8]{1,0:T(8,128)}, u32[]{:S(2)}) %copy-start.2) | copy-done | bytes 280
  3.6 0.0 copy-start.3
  3.6 0.7 %copy-done.3 = s32[256,3]{0,1:T(4,128)S(1)} copy-done((s32[256,3]{0,1:T(4,128)S(1)}, s32[256,3]{0,1:T(4,128)}, u32[]{:S(2)}) %copy-start.3) | copy-done | bytes 3096
  4.3 18.3 %shard_map.77 = (f32[8,8192]{1,0:T(8,128)S(1)}, bf16[8,8192]{1,0:T(8,128)(2,1)S(1)}) custom-call(bf16[8,8192]{1,0:T(8,128)(2,1)S(1)} %copy-done, f32[8]{0:T(128)S(1)} %copy-done.4, f32[8]{0:T(128)S(1)} %copy-done.5, f32[8,80]{1,0:T(8,128)S(1)} %copy-done.1, s32[8,8]{1,0:T(8,128)S(1)} %copy-done.2, s32[3,256]{1,0:T(4,128)S(1)} %bitcast.1), custom_call_target="tpu_custom_call" | custom-call | tf_op jit(solution)/shard_map/pallas_call | solution.py:296
  22.6 0.7 %copy.10 = f32[8,8192]{1,0:T(8,128)} copy(f32[8,8192]{1,0:T(8,128)S(1)} %get-tuple-element.4) | data formatting | bytes 524288
  23.3 0.7 %copy.11 = bf16[8,8192]{1,0:T(8,128)(2,1)} copy(bf16[8,8192]{1,0:T(8,128)(2,1)S(1)} %get-tuple-element.5) | data formatting | bytes 262144
Async XLA Ops:
  0.6 0.7 %copy-start.5 = (f32[8]{0:T(128)S(1)}, f32[8]{0:T(128)}, u32[]{:S(2)}) copy-start(f32[8]{0:T(128)} %shift_ref.1) | copy-start | bytes 100
  0.6 0.7 %copy-start.4 = (f32[8]{0:T(128)S(1)}, f32[8]{0:T(128)}, u32[]{:S(2)}) copy-start(f32[8]{0:T(128)} %conf_ref.1) | copy-start | bytes 100
  1.3 0.9 %copy-start = (bf16[8,8192]{1,0:T(8,128)(2,1)S(1)}, bf16[8,8192]{1,0:T(8,128)(2,1)}, u32[]{:S(2)}) copy-start(bf16[8,8192]{1,0:T(8,128)(2,1)} %phi_ref.1) | copy-start | bytes 393220
  2.2 0.7 %copy-start.1 = (f32[8,80]{1,0:T(8,128)S(1)}, f32[8,80]{1,0:T(8,128)}, u32[]{:S(2)}) copy-start(f32[8,80]{1,0:T(8,128)} %kern_ref.1) | copy-start | bytes 7684
  2.9 0.7 %copy-start.2 = (s32[8,8]{1,0:T(8,128)S(1)}, s32[8,8]{1,0:T(8,128)}, u32[]{:S(2)}) copy-start(s32[8,8]{1,0:T(8,128)} %margins_ref.1) | copy-start | bytes 772
  3.6 0.7 %copy-start.3 = (s32[256,3]{0,1:T(4,128)S(1)}, s32[256,3]{0,1:T(4,128)}, u32[]{:S(2)}) copy-start(s32[256,3]{0,1:T(4,128)} %param.11) | copy-start | bytes 9220

commit v2 on v1

--- a/solution.py
+++ b/solution.py
@@ -14,7 +14,7 @@
 YL = LANES // BZ
 YT = BY // YL
 ROWS = BX * YT
-CHUNKS = 2
+CHUNKS = 4
 MESH = pl.DeviceIdType.MESH
 
 
@@ -55,33 +55,46 @@
 def kernel(
     groups,
     devs,
-    phi_ref,
-    conf_ref,
-    shift_ref,
-    kern_ref,
-    margins_ref,
-    offsets_ref,
-    grad_ref,
-    upd_ref,
-    gath,
-    flat,
-    work,
-    masks,
-    cols,
-    send_sem,
-    recv_sem,
-    halo_send,
+    phi_hbm,
+    conf_hbm,
+    shift_hbm,
+    kern_hbm,
+    margins_hbm,
+    offsets_hbm,
+    change_hbm,
+    scale_hbm,
+    *scratch,
 ):
+    pieces = scratch[:CHUNKS]
+    phi_ref, change, scale_ref, flat, work, masks = scratch[CHUNKS : CHUNKS + 6]
+    conf_ref, shift_ref, kern_ref, margins_ref, offsets_ref, cols = scratch[CHUNKS + 6 : CHUNKS + 12]
+    in_sem, out_sem, send_sem, recv_sem, halo_send = scratch[CHUNKS + 12 :]
     fns = phi_ref.shape[0]
     near = margins_ref.shape[1]
     per_group = devs * fns
     nz = devs // 2
-    part = fns // CHUNKS
+    part = ROWS // CHUNKS
     gi = lax.axis_index("grp")
     me = lax.axis_index("dev")
     core, z = me % 2, me // 2
     sib = me + 1 - 2 * core
     base = (gi * devs + me) * fns
+
+    copies = [
+        pltpu.make_async_copy(src, dst, in_sem.at[i])
+        for i, (src, dst) in enumerate(
+            (
+                (phi_hbm, phi_ref),
+                (offsets_hbm, offsets_ref),
+                (conf_hbm, conf_ref),
+                (shift_hbm, shift_ref),
+                (margins_hbm, margins_ref),
+                (kern_hbm, kern_ref),
+            )
+        )
+    ]
+    for copy in copies:
+        copy.start()
 
     barrier = pltpu.get_barrier_semaphore()
     links = (
@@ -95,6 +108,9 @@
         @pl.when(here)
         def _():
             pl.semaphore_signal(barrier, inc=1, device_id=target, device_id_type=MESH)
+
+    for copy in copies[:4]:
+        copy.wait()
 
     off = [column(fns, lambda f, c=c: offsets_ref[c, base + f]) for c in range(3)]
     conf = column(fns, lambda f: conf_ref[f])
@@ -131,11 +147,13 @@
         flat[pl.ds(t, fns, stride=ROWS), :] = value
 
     tile_roll(lambda t: work[t], put_flat, off[0], off[1], off[2], False)
-    for f in range(fns):
-        gath[me * fns + f] = flat[f * ROWS : (f + 1) * ROWS, :].astype(jnp.bfloat16)
+    for c in range(CHUNKS):
+        for f in range(fns):
+            at = f * ROWS + c * part
+            pieces[c][me * fns + f] = flat[at : at + part, :].astype(jnp.bfloat16)
 
     def piece(block, c):
-        return gath.at[pl.ds(block * fns + c * part, part)]
+        return pieces[c].at[pl.ds(block * fns, fns)]
 
     def line(block, c, way, target):
         return pltpu.make_async_remote_copy(
@@ -179,6 +197,8 @@
         @pl.when(has_below)
         def _():
             halo(False, c).start()
+    for copy in copies[4:]:
+        copy.wait()
 
     row = lax.broadcasted_iota(jnp.int32, (ROWS, LANES), 0)
     lan = lax.broadcasted_iota(jnp.int32, (ROWS, LANES), 1)
@@ -202,6 +222,29 @@
             masks[a * near + k] = jnp.where(keep, kern_ref[a, col], 0.0)
         return carry
 
+    def add_up(c):
+        for block in range(nz):
+            line(2 * block + 1 - core, c, 2, sib).wait_recv()
+
+        @pl.when(has_below)
+        def _():
+            halo(True, c).wait_recv()
+
+        @pl.when(has_above)
+        def _():
+            halo(False, c).wait_recv()
+
+        def one(a, carry):
+            total = None
+            for k in range(near):
+                mask = masks[a * near + k, c * part : (c + 1) * part]
+                term = mask * pieces[c][cols[a * near + k]].astype(jnp.float32)
+                total = term if total is None else total + term
+            flat[pl.ds(pl.multiple_of(a * ROWS + c * part, part), part), :] = total
+            return carry
+
+        lax.fori_loop(0, fns, one, 0)
+
     half = fns // 2
     lax.fori_loop(0, half, make_masks, 0)
 
@@ -228,44 +271,29 @@
                     line(block, c, 1, me - 2).start()
 
                 line(block, c, 2, sib).start()
-        if s == 1:
-            lax.fori_loop(half, fns, make_masks, 0)
-
-    for block in range(nz):
-        for c in range(CHUNKS):
-            line(2 * block + 1 - core, c, 2, sib).wait_recv()
-    for c in range(CHUNKS):
-        @pl.when(has_below)
-        def _():
-            halo(True, c).wait_recv()
-
-        @pl.when(has_above)
-        def _():
-            halo(False, c).wait_recv()
-
-    def add_up(a, carry):
-        total = None
-        for k in range(near):
-            term = masks[a * near + k] * gath[cols[a * near + k]].astype(jnp.float32)
-            total = term if total is None else total + term
-        flat[pl.ds(pl.multiple_of(a * ROWS, ROWS), ROWS), :] = total
-        return carry
-
-    lax.fori_loop(0, fns, add_up, 0)
+
+            if s == 1 and c == CHUNKS - 1:
+                lax.fori_loop(half, fns, make_masks, 0)
+            if s == nz - 1 and c > 0:
+                add_up(c - 1)
+    add_up(CHUNKS - 1)
 
     squares = [zero]
 
-    def put_grad(t, value):
-        grad_ref[:, t * LANES : (t + 1) * LANES] = value
-        stepped = phi_row(t) - 0.5 * value
-        work[t] = stepped
+    def put_change(t, value):
+        value = -0.5 * value
+        change[:, t * LANES : (t + 1) * LANES] = value
+        stepped = phi_row(t) + value
         squares[0] = squares[0] + stepped * stepped
 
-    tile_roll(lambda t: flat[pl.ds(t, fns, stride=ROWS), :], put_grad, off[0], off[1], off[2], True)
+    tile_roll(lambda t: flat[pl.ds(t, fns, stride=ROWS), :], put_change, off[0], off[1], off[2], True)
+    change_out = pltpu.make_async_copy(change, change_hbm, out_sem.at[0])
+    change_out.start()
     mean = jnp.sum(squares[0], axis=1, keepdims=True) / (ROWS * LANES)
-    scale = lax.rsqrt(mean + 1e-06)
-    for t in range(ROWS):
-        upd_ref[:, t * LANES : (t + 1) * LANES] = (work[t] * scale).astype(jnp.bfloat16)
+    scale = jnp.where(lane == lax.broadcasted_iota(jnp.int32, shape, 0), lax.rsqrt(mean + 1e-06), 0.0)
+    scale_ref[...] = jnp.sum(scale, axis=0)[:fns]
+    scale_out = pltpu.make_async_copy(scale_ref, scale_hbm, out_sem.at[1])
+    scale_out.start()
 
     for c in range(CHUNKS):
         for block in range(nz):
@@ -286,35 +314,49 @@
         @pl.when(has_below)
         def _():
             halo(False, c).wait_send()
+    change_out.wait()
+    scale_out.wait()
 
 
 def on_device(groups, devs, phi, conf, shift_energy, kern, margins, offsets):
     fns, cells = phi.shape
     near = margins.shape[1]
-    vmem = pl.BlockSpec(memory_space=pltpu.VMEM)
-    smem = pl.BlockSpec(memory_space=pltpu.SMEM)
-    return pl.pallas_call(
+    hbm = pl.BlockSpec(memory_space=pltpu.HBM)
+    change, scale = pl.pallas_call(
         functools.partial(kernel, groups, devs),
         out_shape=(
             jax.ShapeDtypeStruct((fns, cells), jnp.float32),
-            jax.ShapeDtypeStruct((fns, cells), jnp.bfloat16),
+            jax.ShapeDtypeStruct((fns,), jnp.float32),
         ),
-        in_specs=[vmem, smem, smem, smem, smem, smem],
-        out_specs=(vmem, vmem),
-        scratch_shapes=[
-            pltpu.VMEM(((devs + 2) * fns, ROWS, LANES), jnp.bfloat16),
+        in_specs=[hbm] * 6,
+        out_specs=(hbm, hbm),
+        scratch_shapes=[pltpu.VMEM(((devs + 2) * fns, ROWS // CHUNKS, LANES), jnp.bfloat16)] * CHUNKS
+        + [
+            pltpu.VMEM((fns, cells), jnp.bfloat16),
+            pltpu.VMEM((fns, cells), jnp.float32),
+            pltpu.VMEM((fns,), jnp.float32),
             pltpu.VMEM((fns * ROWS, LANES), jnp.float32),
             pltpu.VMEM((ROWS, fns, LANES), jnp.float32),
             pltpu.VMEM((fns * near, ROWS, LANES), jnp.float32),
+            pltpu.SMEM(conf.shape, jnp.float32),
+            pltpu.SMEM(shift_energy.shape, jnp.float32),
+            pltpu.SMEM(kern.shape, jnp.float32),
+            pltpu.SMEM(margins.shape, jnp.int32),
+            pltpu.SMEM(offsets.shape[::-1], jnp.int32),
             pltpu.SMEM((fns * near,), jnp.int32),
+            pltpu.SemaphoreType.DMA((6,)),
+            pltpu.SemaphoreType.DMA((2,)),
             pltpu.SemaphoreType.DMA((3, devs, CHUNKS)),
             pltpu.SemaphoreType.DMA((devs + 2, CHUNKS)),
             pltpu.SemaphoreType.DMA((2, CHUNKS)),
         ],
         compiler_params=pltpu.CompilerParams(
-            collective_id=0, has_side_effects=True, vmem_limit_bytes=32 * 1024 * 1024
+            collective_id=0, has_side_effects=True, vmem_limit_bytes=60 * 1024 * 1024
         ),
     )(phi, conf, shift_energy, kern, margins, offsets.T)
+    gradient = -2.0 * change
+    stepped = phi.astype(jnp.float32) + change
+    return (gradient, (stepped * scale[:, None]).astype(jnp.bfloat16))
 
 
 def solution(mesh):

time: 24.2 us -> 22 us (0.909)
  the two profiles are of different devices: /device:TPU:1 before, /device:TPU:0 now
where the time goes in v2:
time: 22 us; the launch traced here: 21.8 us
  Pallas kernels  18.8 us (85%)
  other arithmetic  1.71 us (8%)
  local copies, waits for them, and re-layouts  0.66 us (3%)
  between operations  0.66 us (3%)
    pallas_call x1, Pallas kernels, on_device(): pl.pallas_call(functools.partial(kernel, groups, devs), out_shape=(jax.Sh...  18.8 us
    convert_element_type x1, other arithmetic, on_device(): return (gradient, (stepped * scale[:, None]).astype(jnp.bfloat16))  1.71 us
    unnamed x4, local copies, waits for them, and re-layouts  0.66 us

profile of v2, /device:TPU:0, one launch (start us, length us, event | category | flops | bytes accessed | tf_op | source)
XLA Modules:
  0.0 21.8 jit_solution(2672732670692204326)
XLA Ops:
  0.6 0.0 copy-start
  0.6 18.8 %shard_map.77 = (f32[8,8192]{1,0:T(8,128)}, f32[8]{0:T(128)}) custom-call(bf16[8,8192]{1,0:T(8,128)(2,1)} %phi_hbm.1, f32[8]{0:T(128)} %conf_hbm.1, f32[8]{0:T(128)} %shift_hbm.1, f32[8,80]{1,0:T(8,128)} %kern_hbm.1, s32[8,8]{1,0:T(8,128)} %margins_hbm.1, s32[3,256]{1,0:T(4,128)} %bitcast.1), custom_call_target="tpu_custom_call" | custom-call | tf_op jit(solution)/shard_map/pallas_call | solution.py:325
  19.4 0.0 copy-start.1
  19.5 0.0 copy-done
  19.5 0.7 %copy-done.1 = f32[8]{0:T(128)S(1)} copy-done((f32[8]{0:T(128)S(1)}, f32[8]{0:T(128)}, u32[]{:S(2)}) %copy-start.1) | copy-done | bytes 56
  20.1 1.7 %multiply_convert_fusion = (bf16[8,8192]{1,0:T(8,128)(2,1)}, f32[8,8192]{1,0:T(8,128)}) fusion(f32[8,8192]{1,0:T(8,128)} %get-tuple-element.4, bf16[8,8192]{1,0:T(8,128)(2,1)S(1)} %copy-done, f32[8]{0:T(128)S(1)} %copy-done.1), kind=kLoop, calls=%fused_computation | loop fusion | flops 327680 | bytes 786464 | tf_op jit(solution)/shard_map/convert_element_type | solution.py:359
Async XLA Ops:
  0.6 18.8 %copy-start = (bf16[8,8192]{1,0:T(8,128)(2,1)S(1)}, bf16[8,8192]{1,0:T(8,128)(2,1)}, u32[]{:S(2)}) copy-start(bf16[8,8192]{1,0:T(8,128)(2,1)} %phi_hbm.1) | copy-start | bytes 393220
  19.4 0.7 %copy-start.1 = (f32[8]{0:T(128)S(1)}, f32[8]{0:T(128)}, u32[]{:S(2)}) copy-start(f32[8]{0:T(128)} %get-tuple-element.5) | copy-start | bytes 100

commit v3 on v2

--- a/solution.py
+++ b/solution.py
@@ -52,23 +52,10 @@
             put(x * YT + t, rows[x])
 
 
-def kernel(
-    groups,
-    devs,
-    phi_hbm,
-    conf_hbm,
-    shift_hbm,
-    kern_hbm,
-    margins_hbm,
-    offsets_hbm,
-    change_hbm,
-    scale_hbm,
-    *scratch,
-):
+def gather_kernel(groups, devs, phi_hbm, conf_hbm, shift_hbm, kern_hbm, margins_hbm, offsets_hbm, sums_ref, off_ref, phi_ref, *scratch):
     pieces = scratch[:CHUNKS]
-    phi_ref, change, scale_ref, flat, work, masks = scratch[CHUNKS : CHUNKS + 6]
-    conf_ref, shift_ref, kern_ref, margins_ref, offsets_ref, cols = scratch[CHUNKS + 6 : CHUNKS + 12]
-    in_sem, out_sem, send_sem, recv_sem, halo_send = scratch[CHUNKS + 12 :]
+    flat, work, masks, conf_ref, shift_ref, kern_ref, margins_ref, offsets_ref, cols = scratch[CHUNKS : CHUNKS + 9]
+    in_sem, send_sem, recv_sem, halo_send = scratch[CHUNKS + 9 :]
     fns = phi_ref.shape[0]
     near = margins_ref.shape[1]
     per_group = devs * fns
@@ -113,6 +100,8 @@
         copy.wait()
 
     off = [column(fns, lambda f, c=c: offsets_ref[c, base + f]) for c in range(3)]
+    for c in range(3):
+        off_ref[c] = off[c]
     conf = column(fns, lambda f: conf_ref[f])
     shift = column(fns, lambda f: shift_ref[f])
     shape = (fns, LANES)
@@ -240,7 +229,7 @@
                 mask = masks[a * near + k, c * part : (c + 1) * part]
                 term = mask * pieces[c][cols[a * near + k]].astype(jnp.float32)
                 total = term if total is None else total + term
-            flat[pl.ds(pl.multiple_of(a * ROWS + c * part, part), part), :] = total
+            sums_ref[pl.ds(pl.multiple_of(a * ROWS + c * part, part), part), :] = total
             return carry
 
         lax.fori_loop(0, fns, one, 0)
@@ -278,23 +267,6 @@
                 add_up(c - 1)
     add_up(CHUNKS - 1)
 
-    squares = [zero]
-
-    def put_change(t, value):
-        value = -0.5 * value
-        change[:, t * LANES : (t + 1) * LANES] = value
-        stepped = phi_row(t) + value
-        squares[0] = squares[0] + stepped * stepped
-
-    tile_roll(lambda t: flat[pl.ds(t, fns, stride=ROWS), :], put_change, off[0], off[1], off[2], True)
-    change_out = pltpu.make_async_copy(change, change_hbm, out_sem.at[0])
-    change_out.start()
-    mean = jnp.sum(squares[0], axis=1, keepdims=True) / (ROWS * LANES)
-    scale = jnp.where(lane == lax.broadcasted_iota(jnp.int32, shape, 0), lax.rsqrt(mean + 1e-06), 0.0)
-    scale_ref[...] = jnp.sum(scale, axis=0)[:fns]
-    scale_out = pltpu.make_async_copy(scale_ref, scale_hbm, out_sem.at[1])
-    scale_out.start()
-
     for c in range(CHUNKS):
         for block in range(nz):
             line(2 * block + core, c, 2, sib).wait_send()
@@ -314,27 +286,49 @@
         @pl.when(has_below)
         def _():
             halo(False, c).wait_send()
-    change_out.wait()
-    scale_out.wait()
+
+
+def step_kernel(sums_ref, off_ref, phi_ref, grad_hbm, upd_hbm, grad, upd, work, out_sem):
+    fns = phi_ref.shape[0]
+    squares = [jnp.zeros((fns, LANES), jnp.float32)]
+
+    def put_grad(t, value):
+        grad[:, t * LANES : (t + 1) * LANES] = value
+        stepped = phi_ref[:, t * LANES : (t + 1) * LANES].astype(jnp.float32) - 0.5 * value
+        work[t] = stepped
+        squares[0] = squares[0] + stepped * stepped
+
+    tile_roll(
+        lambda t: sums_ref[pl.ds(t, fns, stride=ROWS), :], put_grad, off_ref[0], off_ref[1], off_ref[2], True
+    )
+    grad_out = pltpu.make_async_copy(grad, grad_hbm, out_sem.at[0])
+    grad_out.start()
+    mean = jnp.sum(squares[0], axis=1, keepdims=True) / (ROWS * LANES)
+    scale = lax.rsqrt(mean + 1e-06)
+    for t in range(ROWS):
+        upd[:, t * LANES : (t + 1) * LANES] = (work[t] * scale).astype(jnp.bfloat16)
+    upd_out = pltpu.make_async_copy(upd, upd_hbm, out_sem.at[1])
+    upd_out.start()
+    grad_out.wait()
+    upd_out.wait()
 
 
 def on_device(groups, devs, phi, conf, shift_energy, kern, margins, offsets):
     fns, cells = phi.shape
     near = margins.shape[1]
+    vmem = pl.BlockSpec(memory_space=pltpu.VMEM)
     hbm = pl.BlockSpec(memory_space=pltpu.HBM)
-    change, scale = pl.pallas_call(
-        functools.partial(kernel, groups, devs),
+    sums, off, held = pl.pallas_call(
+        functools.partial(gather_kernel, groups, devs),
         out_shape=(
-            jax.ShapeDtypeStruct((fns, cells), jnp.float32),
-            jax.ShapeDtypeStruct((fns,), jnp.float32),
+            jax.ShapeDtypeStruct((fns * ROWS, LANES), jnp.float32),
+            jax.ShapeDtypeStruct((3, fns, LANES), jnp.int32),
+            jax.ShapeDtypeStruct((fns, cells), jnp.bfloat16),
         ),
         in_specs=[hbm] * 6,
-        out_specs=(hbm, hbm),
+        out_specs=(vmem, vmem, vmem),
         scratch_shapes=[pltpu.VMEM(((devs + 2) * fns, ROWS // CHUNKS, LANES), jnp.bfloat16)] * CHUNKS
         + [
-            pltpu.VMEM((fns, cells), jnp.bfloat16),
-            pltpu.VMEM((fns, cells), jnp.float32),
-            pltpu.VMEM((fns,), jnp.float32),
             pltpu.VMEM((fns * ROWS, LANES), jnp.float32),
             pltpu.VMEM((ROWS, fns, LANES), jnp.float32),
             pltpu.VMEM((fns * near, ROWS, LANES), jnp.float32),
@@ -345,18 +339,33 @@
             pltpu.SMEM(offsets.shape[::-1], jnp.int32),
             pltpu.SMEM((fns * near,), jnp.int32),
             pltpu.SemaphoreType.DMA((6,)),
-            pltpu.SemaphoreType.DMA((2,)),
             pltpu.SemaphoreType.DMA((3, devs, CHUNKS)),
             pltpu.SemaphoreType.DMA((devs + 2, CHUNKS)),
             pltpu.SemaphoreType.DMA((2, CHUNKS)),
         ],
         compiler_params=pltpu.CompilerParams(
-            collective_id=0, has_side_effects=True, vmem_limit_bytes=60 * 1024 * 1024
+            collective_id=0, has_side_effects=True, vmem_limit_bytes=32 * 1024 * 1024
         ),
-    )(phi, conf, shift_energy, kern, margins, offsets.T)
-    gradient = -2.0 * change
-    stepped = phi.astype(jnp.float32) + change
-    return (gradient, (stepped * scale[:, None]).astype(jnp.bfloat16))
+    )(*(
+        pltpu.with_memory_space_constraint(array, pltpu.HBM)
+        for array in (phi, conf, shift_energy, kern, margins, offsets.T)
+    ))
+    return pl.pallas_call(
+        step_kernel,
+        out_shape=(
+            jax.ShapeDtypeStruct((fns, cells), jnp.float32),
+            jax.ShapeDtypeStruct((fns, cells), jnp.bfloat16),
+        ),
+        in_specs=[vmem, vmem, vmem],
+        out_specs=(hbm, hbm),
+        scratch_shapes=[
+            pltpu.VMEM((fns, cells), jnp.float32),
+            pltpu.VMEM((fns, cells), jnp.bfloat16),
+            pltpu.VMEM((ROWS, fns, LANES), jnp.float32),
+            pltpu.SemaphoreType.DMA((2,)),
+        ],
+        compiler_params=pltpu.CompilerParams(vmem_limit_bytes=16 * 1024 * 1024),
+    )(sums, off, held)
 
 
 def solution(mesh):

time: 22 us -> 19.7 us (0.90)
  other arithmetic: 1.71 us -> 0 us
  local copies, waits for them, and re-layouts: 0.66 us -> 0 us
    convert_element_type x1 -> x0, other arithmetic: 1.71 us -> none  [on_device(): return (gradient, (stepped * scale[:, None]).astype(jnp.bfloat16))]
    unnamed x4 -> x0, local copies, waits for them, and re-layouts: 0.66 us -> none
    pallas_call x1 -> x2, Pallas kernels: 18.8 us -> 18.9 us  [the longest x1 17.8 us: on_device(): pl.pallas_call(functools.partial(gather_kernel, groups, devs), out_shape=...]
where the time goes in v3:
time: 19.7 us; the launch traced here: 19.6 us
  Pallas kernels  18.9 us (96%)
  between operations  0.64 us (3%)
    pallas_call x1, Pallas kernels, on_device(): pl.pallas_call(functools.partial(gather_kernel, groups, devs), out_shape=...  17.8 us
    pallas_call x1, Pallas kernels, on_device(): pl.pallas_call(step_kernel, out_shape=(jax.ShapeDtypeStruct((fns, cells),...  1.09 us

profile of v3, /device:TPU:0, one launch (start us, length us, event | category | flops | bytes accessed | tf_op | source)
XLA Modules:
  0.0 19.6 jit_solution(1235916233364363656)
XLA Ops:
  0.6 17.8 %shard_map.77 = (f32[512,128]{1,0:T(8,128)S(1)}, s32[3,8,128]{2,1,0:T(8,128)S(1)}, bf16[8,8192]{1,0:T(8,128)(2,1)S(1)}) custom-call(bf16[8,8192]{1,0:T(8,128)(2,1)} %phi_hbm.1, f32[8]{0:T(128)} %conf_hbm.1, f32[8]{0:T(128)} %shift_hbm.1, f32[8,80]{1,0:T(8,128)} %kern_hbm.1, s32[8,8]{1,0:T(8,128)} %margins_hbm.1, s32[3,256]{1,0:T(4,128)} %bitcast.1), custom_call_target="tpu_custom_call" | custom-call | tf_op jit(solution)/shard_map/pallas_call | solution.py:321
  18.5 1.1 %shard_map.78 = (f32[8,8192]{1,0:T(8,128)}, bf16[8,8192]{1,0:T(8,128)(2,1)}) custom-call(f32[512,128]{1,0:T(8,128)S(1)} %get-tuple-element.5.sums_ref, s32[3,8,128]{2,1,0:T(8,128)S(1)} %get-tuple-element.6.off_ref, bf16[8,8192]{1,0:T(8,128)(2,1)S(1)} %get-tuple-element.7.phi_ref), custom_call_target="tpu_custom_call" | custom-call | tf_op jit(solution)/shard_map/pallas_call | solution.py:353

commit v4 on v3

--- a/solution.py
+++ b/solution.py
@@ -55,7 +55,8 @@
 def gather_kernel(groups, devs, phi_hbm, conf_hbm, shift_hbm, kern_hbm, margins_hbm, offsets_hbm, sums_ref, off_ref, phi_ref, *scratch):
     pieces = scratch[:CHUNKS]
     flat, work, masks, conf_ref, shift_ref, kern_ref, margins_ref, offsets_ref, cols = scratch[CHUNKS : CHUNKS + 9]
-    in_sem, send_sem, recv_sem, halo_send = scratch[CHUNKS + 9 :]
+    far_margins_in, far_kern_in, far_margins, far_kern, far_masks, far_cols, share_out, share_in = scratch[CHUNKS + 9 : CHUNKS + 17]
+    in_sem, send_sem, recv_sem, halo_send, far_send, far_recv, far_copy, share_send, share_recv = scratch[CHUNKS + 17 :]
     fns = phi_ref.shape[0]
     near = margins_ref.shape[1]
     per_group = devs * fns
@@ -66,6 +67,11 @@
     core, z = me % 2, me // 2
     sib = me + 1 - 2 * core
     base = (gi * devs + me) * fns
+    at_end = (z == 0) | (z == nz - 1)
+    helps = (z == 1) | (z == nz - 2)
+    helped = jnp.where(z == 1, me - 2, me + 2)
+    helper = jnp.where(z == 0, me + 2, me - 2)
+    helped_base = (gi * devs + helped) * fns
 
     copies = [
         pltpu.make_async_copy(src, dst, in_sem.at[i])
@@ -167,7 +173,34 @@
     has_left, has_right = z > 0, z < nz - 1
     has_below, has_above = gi > 0, gi < groups - 1
 
+    def to_helper(i):
+        src, dst = ((margins_hbm, far_margins_in), (kern_hbm, far_kern_in))[i]
+        return pltpu.make_async_remote_copy(
+            src_ref=src,
+            dst_ref=dst,
+            send_sem=far_send.at[i],
+            recv_sem=far_recv.at[i],
+            device_id=(gi, helper),
+            device_id_type=MESH,
+        )
+
+    def to_helped(c):
+        return pltpu.make_async_remote_copy(
+            src_ref=share_out.at[c],
+            dst_ref=share_in.at[c],
+            send_sem=share_send.at[c],
+            recv_sem=share_recv.at[c],
+            device_id=(gi, helped),
+            device_id_type=MESH,
+        )
+
     pl.semaphore_wait(barrier, 1 + sum(jnp.where(h, 1, 0) for h, _ in links[1:]))
+
+    @pl.when(at_end)
+    def _():
+        for i in range(2):
+            to_helper(i).start()
+
     for c in range(CHUNKS):
         @pl.when(has_right)
         def _():
@@ -193,27 +226,53 @@
     lan = lax.broadcasted_iota(jnp.int32, (ROWS, LANES), 1)
     cell = (row // YT, row % YT * YL + lan // BZ, lan % BZ)
 
-    def make_masks(a, carry):
+    def make_masks(far):
+        rows_of, kern_of, masks_of, cols_of, first = (
+            (far_margins, far_kern, far_masks, far_cols, helped_base)
+            if far
+            else (margins_ref, kern_ref, masks, cols, base)
+        )
+
+        def one(a, carry):
+            for k in range(near):
+                b = rows_of[a, k]
+                gb = b // per_group
+                col = jnp.where(
+                    gb == gi,
+                    b - gb * per_group,
+                    jnp.where(gb == gi - 1, per_group, per_group + fns) + b % fns,
+                )
+                zb = jnp.where(gb == gi, col // (2 * fns), z)
+                if far:
+                    use = (gb == gi) & jnp.where(z == 1, zb >= 2, zb <= nz - 3)
+                else:
+                    use = ((z > 0) | (zb < 2)) & ((z < nz - 1) | (zb > nz - 3))
+                col = jnp.where(use, col, me * fns)
+                cols_of[a * near + k] = col
+                weight = jnp.where(use, kern_of[a, col], 0.0)
+                keep = None
+                for axis in range(3):
+                    oa, ob = offsets_ref[axis, first + a], offsets_ref[axis, b]
+                    out = (cell[axis] < jnp.minimum(oa, ob)) | (cell[axis] >= jnp.maximum(oa, ob))
+                    keep = out if keep is None else keep & out
+                masks_of[a * near + k] = jnp.where(keep, weight, 0.0)
+            return carry
+
+        return one
+
+    def weighted(masks_of, cols_of, a, c):
+        total = None
         for k in range(near):
-            b = margins_ref[a, k]
-            gb = b // per_group
-            col = jnp.where(
-                gb == gi,
-                b - gb * per_group,
-                jnp.where(gb == gi - 1, per_group, per_group + fns) + b % fns,
-            )
-            cols[a * near + k] = col
-            keep = None
-            for axis in range(3):
-                oa, ob = offsets_ref[axis, base + a], offsets_ref[axis, b]
-                out = (cell[axis] < jnp.minimum(oa, ob)) | (cell[axis] >= jnp.maximum(oa, ob))
-                keep = out if keep is None else keep & out
-            masks[a * near + k] = jnp.where(keep, kern_ref[a, col], 0.0)
-        return carry
+            mask = masks_of[a * near + k, c * part : (c + 1) * part]
+            term = mask * pieces[c][cols_of[a * near + k]].astype(jnp.float32)
+            total = term if total is None else total + term
+        return total
 
     def add_up(c):
         for block in range(nz):
-            line(2 * block + 1 - core, c, 2, sib).wait_recv()
+            @pl.when(~at_end | (abs(block - z) <= 1))
+            def _():
+                line(2 * block + 1 - core, c, 2, sib).wait_recv()
 
         @pl.when(has_below)
         def _():
@@ -223,59 +282,92 @@
         def _():
             halo(False, c).wait_recv()
 
+        def one_far(a, carry):
+            share_out[c, a] = weighted(far_masks, far_cols, a, c).astype(jnp.bfloat16)
+            return carry
+
         def one(a, carry):
-            total = None
-            for k in range(near):
-                mask = masks[a * near + k, c * part : (c + 1) * part]
-                term = mask * pieces[c][cols[a * near + k]].astype(jnp.float32)
-                total = term if total is None else total + term
-            sums_ref[pl.ds(pl.multiple_of(a * ROWS + c * part, part), part), :] = total
+            sums_ref[pl.ds(pl.multiple_of(a * ROWS + c * part, part), part), :] = weighted(masks, cols, a, c)
             return carry
 
+        @pl.when(helps)
+        def _():
+            lax.fori_loop(0, fns, one_far, 0)
+            to_helped(c).start()
+
         lax.fori_loop(0, fns, one, 0)
 
     half = fns // 2
-    lax.fori_loop(0, half, make_masks, 0)
-
-    for s in range(1, nz):
+    lax.fori_loop(0, half, make_masks(False), 0)
+
+    for s in range(1, nz - 1):
         for c in range(CHUNKS):
-            @pl.when(z - s >= 0)
+            @pl.when((z - s >= 0) & ((z < nz - 1) | (s == 1)))
             def _():
                 block = me - 2 * s
                 line(block, c, 0, me + 2).wait_recv()
 
-                @pl.when(has_right)
+                @pl.when(z < nz - 2)
                 def _():
                     line(block, c, 0, me + 2).start()
 
                 line(block, c, 2, sib).start()
 
-            @pl.when(z + s < nz)
+            @pl.when((z + s < nz) & ((z > 0) | (s == 1)))
             def _():
                 block = me + 2 * s
                 line(block, c, 1, me - 2).wait_recv()
 
-                @pl.when(has_left)
+                @pl.when(z > 1)
                 def _():
                     line(block, c, 1, me - 2).start()
 
                 line(block, c, 2, sib).start()
 
-            if s == 1 and c == CHUNKS - 1:
-                lax.fori_loop(half, fns, make_masks, 0)
-            if s == nz - 1 and c > 0:
+            if s == 1 and c == 0:
+                lax.fori_loop(half, fns, make_masks(False), 0)
+            if s == 1 and c == 1:
+                @pl.when(helps)
+                def _():
+                    into = [
+                        pltpu.make_async_copy(far_margins_in, far_margins, far_copy.at[0]),
+                        pltpu.make_async_copy(far_kern_in, far_kern, far_copy.at[1]),
+                    ]
+                    for i in range(2):
+                        to_helper(i).wait_recv()
+                        into[i].start()
+                    for i in range(2):
+                        into[i].wait()
+                    lax.fori_loop(0, half, make_masks(True), 0)
+
+            if s == 1 and c == 2:
+                @pl.when(helps)
+                def _():
+                    lax.fori_loop(half, fns, make_masks(True), 0)
+
+            if s == nz - 2 and c > 0:
                 add_up(c - 1)
     add_up(CHUNKS - 1)
 
+    @pl.when(at_end)
+    def _():
+        for c in range(CHUNKS):
+            to_helped(c).wait_recv()
+            for a in range(fns):
+                at = a * ROWS + c * part
+                sums_ref[at : at + part, :] = sums_ref[at : at + part, :] + share_in[c, a].astype(jnp.float32)
+
     for c in range(CHUNKS):
         for block in range(nz):
-            line(2 * block + core, c, 2, sib).wait_send()
-
-            @pl.when(has_right & (block <= z))
+            @pl.when(~at_end | (abs(block - z) <= 1))
+            def _():
+                line(2 * block + core, c, 2, sib).wait_send()
+
+            @pl.when(has_right & ((block == z) | ((block < z) & (z < nz - 2))))
             def _():
                 line(2 * block + core, c, 0, me + 2).wait_send()
 
-            @pl.when(has_left & (block >= z))
+            @pl.when(has_left & ((block == z) | ((block > z) & (z > 1))))
             def _():
                 line(2 * block + core, c, 1, me - 2).wait_send()
 
@@ -286,6 +378,15 @@
         @pl.when(has_below)
         def _():
             halo(False, c).wait_send()
+
+        @pl.when(helps)
+        def _():
+            to_helped(c).wait_send()
+
+    @pl.when(at_end)
+    def _():
+        for i in range(2):
+            to_helper(i).wait_send()
 
 
 def step_kernel(sums_ref, off_ref, phi_ref, grad_hbm, upd_hbm, grad, upd, work, out_sem):
@@ -338,10 +439,23 @@
             pltpu.SMEM(margins.shape, jnp.int32),
             pltpu.SMEM(offsets.shape[::-1], jnp.int32),
             pltpu.SMEM((fns * near,), jnp.int32),
+            pltpu.VMEM(margins.shape, jnp.int32),
+            pltpu.VMEM(kern.shape, jnp.float32),
+            pltpu.SMEM(margins.shape, jnp.int32),
+            pltpu.SMEM(kern.shape, jnp.float32),
+            pltpu.VMEM((fns * near, ROWS, LANES), jnp.float32),
+            pltpu.SMEM((fns * near,), jnp.int32),
+            pltpu.VMEM((CHUNKS, fns, ROWS // CHUNKS, LANES), jnp.bfloat16),
+            pltpu.VMEM((CHUNKS, fns, ROWS // CHUNKS, LANES), jnp.bfloat16),
             pltpu.SemaphoreType.DMA((6,)),
             pltpu.SemaphoreType.DMA((3, devs, CHUNKS)),
             pltpu.SemaphoreType.DMA((devs + 2, CHUNKS)),
             pltpu.SemaphoreType.DMA((2, CHUNKS)),
+            pltpu.SemaphoreType.DMA((2,)),
+            pltpu.SemaphoreType.DMA((2,)),
+            pltpu.SemaphoreType.DMA((2,)),
+            pltpu.SemaphoreType.DMA((CHUNKS,)),
+            pltpu.SemaphoreType.DMA((CHUNKS,)),
         ],
         compiler_params=pltpu.CompilerParams(
             collective_id=0, has_side_effects=True, vmem_limit_bytes=32 * 1024 * 1024

time: 19.7 us -> 21.8 us (1.11)
  Pallas kernels: 18.9 us -> 21 us
    pallas_call x1, Pallas kernels: 17.8 us -> 19.9 us  [on_device(): pl.pallas_call(functools.partial(gather_kernel, groups, devs), out_shape=...]
where the time goes in v4:
time: 21.8 us; the launch traced here: 21.6 us
  Pallas kernels  21 us (96%)
  between operations  0.64 us (3%)
    pallas_call x1, Pallas kernels, on_device(): pl.pallas_call(functools.partial(gather_kernel, groups, devs), out_shape=...  19.9 us
    pallas_call x1, Pallas kernels, on_device(): pl.pallas_call(step_kernel, out_shape=(jax.ShapeDtypeStruct((fns, cells),...  1.09 us

profile of v4, /device:TPU:0, one launch (start us, length us, event | category | flops | bytes accessed | tf_op | source)
XLA Modules:
  0.0 21.6 jit_solution(6855663616915705684)
XLA Ops:
  0.6 19.9 %shard_map.77 = (f32[512,128]{1,0:T(8,128)S(1)}, s32[3,8,128]{2,1,0:T(8,128)S(1)}, bf16[8,8192]{1,0:T(8,128)(2,1)S(1)}) custom-call(bf16[8,8192]{1,0:T(8,128)(2,1)} %phi_hbm.1, f32[8]{0:T(128)} %conf_hbm.1, f32[8]{0:T(128)} %shift_hbm.1, f32[8,80]{1,0:T(8,128)} %kern_hbm.1, s32[8,8]{1,0:T(8,128)} %margins_hbm.1, s32[3,256]{1,0:T(4,128)} %bitcast.1), custom_call_target="tpu_custom_call" | custom-call | tf_op jit(solution)/shard_map/pallas_call | solution.py:422
  20.6 1.1 %shard_map.78 = (f32[8,8192]{1,0:T(8,128)}, bf16[8,8192]{1,0:T(8,128)(2,1)}) custom-call(f32[512,128]{1,0:T(8,128)S(1)} %get-tuple-element.5.sums_ref, s32[3,8,128]{2,1,0:T(8,128)S(1)} %get-tuple-element.6.off_ref, bf16[8,8192]{1,0:T(8,128)(2,1)S(1)} %get-tuple-element.7.phi_ref), custom_call_target="tpu_custom_call" | custom-call | tf_op jit(solution)/shard_map/pallas_call | solution.py:467

commit v5 on v4

--- a/solution.py
+++ b/solution.py
@@ -15,6 +15,8 @@
 YT = BY // YL
 ROWS = BX * YT
 CHUNKS = 4
+TOP = 8
+MASKED = TOP * YT
 MESH = pl.DeviceIdType.MESH
 
 
@@ -113,30 +115,29 @@
     shape = (fns, LANES)
     lane = lax.broadcasted_iota(jnp.int32, shape, 1)
     yl, zz = lane // BZ, lane % BZ
-    zf = (zz.astype(jnp.float32) - (BZ - 1) / 2.0) / BZ
     zero = jnp.zeros(shape, jnp.float32)
 
     def phi_row(t):
         return phi_ref[:, t * LANES : (t + 1) * LANES].astype(jnp.float32)
 
+    zf = (zz.astype(jnp.float32) - (BZ - 1) / 2.0) / BZ
+    yf = [((yl + t * YL).astype(jnp.float32) - (BY - 1) / 2.0) / BY for t in range(YT)]
+    plane_coef = [conf * (y * y + zf * zf) - shift + 3.0 for y in yf]
+    first_y, last_y, first_z, last_z = yl == 0, yl == YL - 1, zz == 0, zz == BZ - 1
+    before, rows = [zero] * YT, [phi_row(t) for t in range(YT)]
     for x in range(BX):
-        xf = ((x - (BX - 1) / 2.0) / BX) ** 2
-        rows = [phi_row(x * YT + t) for t in range(YT)]
+        after = [phi_row((x + 1) * YT + t) for t in range(YT)] if x < BX - 1 else [zero] * YT
         ups = [pltpu.roll(r, LANES - BZ, 1) for r in rows] + [zero]
         downs = [zero] + [pltpu.roll(r, BZ, 1) for r in rows]
+        x_coef = conf * ((x - (BX - 1) / 2.0) / BX) ** 2
         for t in range(YT):
             field = rows[t]
-            lap = phi_row((x + 1) * YT + t) if x < BX - 1 else zero
-            if x > 0:
-                lap = lap + phi_row((x - 1) * YT + t)
-            lap = lap + jnp.where(yl < YL - 1, ups[t], ups[t + 1])
-            lap = lap + jnp.where(yl > 0, downs[t + 1], downs[t])
-            lap = lap + jnp.where(zz < BZ - 1, pltpu.roll(field, LANES - 1, 1), 0.0)
-            lap = lap + jnp.where(zz > 0, pltpu.roll(field, 1, 1), 0.0)
-            lap = lap - 6.0 * field
-            yf = ((yl + t * YL).astype(jnp.float32) - (BY - 1) / 2.0) / BY
-            radius = xf + yf * yf + zf * zf
-            work[x * YT + t] = -0.5 * lap + conf * radius * field - shift * field
+            near_x = before[t] + after[t]
+            near_y = jnp.where(last_y, ups[t + 1], ups[t]) + jnp.where(first_y, downs[t], downs[t + 1])
+            near_z = jnp.where(last_z, 0.0, pltpu.roll(field, LANES - 1, 1))
+            near_z = near_z + jnp.where(first_z, 0.0, pltpu.roll(field, 1, 1))
+            work[x * YT + t] = (plane_coef[t] + x_coef) * field - 0.5 * (near_x + near_y + near_z)
+        before, rows = rows, after
 
     def put_flat(t, value):
         flat[pl.ds(t, fns, stride=ROWS), :] = value
@@ -222,9 +223,15 @@
     for copy in copies[4:]:
         copy.wait()
 
-    row = lax.broadcasted_iota(jnp.int32, (ROWS, LANES), 0)
-    lan = lax.broadcasted_iota(jnp.int32, (ROWS, LANES), 1)
-    cell = (row // YT, row % YT * YL + lan // BZ, lan % BZ)
+    sub = lax.broadcasted_iota(jnp.int32, (2 * YT, LANES), 0)
+    lan = lax.broadcasted_iota(jnp.int32, (2 * YT, LANES), 1)
+    y_cell, z_cell = sub % YT * YL + lan // BZ, lan % BZ
+    x_cells = [sub // YT + 2 * i for i in range(TOP // 2)]
+    group_first = gi * per_group
+
+    def sides(at):
+        ox, oy, oz = (offsets_ref[axis, at] for axis in range(3))
+        return [x < ox for x in x_cells], y_cell < oy, z_cell < oz
 
     def make_masks(far):
         rows_of, kern_of, masks_of, cols_of, first = (
@@ -234,36 +241,38 @@
         )
 
         def one(a, carry):
+            ax, ay, az = sides(first + a)
             for k in range(near):
                 b = rows_of[a, k]
-                gb = b // per_group
-                col = jnp.where(
-                    gb == gi,
-                    b - gb * per_group,
-                    jnp.where(gb == gi - 1, per_group, per_group + fns) + b % fns,
-                )
-                zb = jnp.where(gb == gi, col // (2 * fns), z)
+                col = b - group_first
+                inside = (col >= 0) & (col < per_group)
+                beyond = jnp.where(col < 0, per_group, per_group + fns) + lax.rem(b, fns)
+                col = jnp.where(inside, col, beyond)
                 if far:
-                    use = (gb == gi) & jnp.where(z == 1, zb >= 2, zb <= nz - 3)
+                    use = inside & jnp.where(z == 1, col >= 4 * fns, col < 2 * (nz - 2) * fns)
                 else:
-                    use = ((z > 0) | (zb < 2)) & ((z < nz - 1) | (zb > nz - 3))
+                    use = ~inside | (((z > 0) | (col < 4 * fns)) & ((z < nz - 1) | (col >= 2 * (nz - 2) * fns)))
                 col = jnp.where(use, col, me * fns)
                 cols_of[a * near + k] = col
                 weight = jnp.where(use, kern_of[a, col], 0.0)
-                keep = None
-                for axis in range(3):
-                    oa, ob = offsets_ref[axis, first + a], offsets_ref[axis, b]
-                    out = (cell[axis] < jnp.minimum(oa, ob)) | (cell[axis] >= jnp.maximum(oa, ob))
-                    keep = out if keep is None else keep & out
-                masks_of[a * near + k] = jnp.where(keep, weight, 0.0)
+                bx, by, bz = sides(b)
+                rest = jnp.where((ay ^ by) | (az ^ bz), 0.0, weight)
+                for i in range(TOP // 2):
+                    masks_of[a * near + k, 2 * YT * i : 2 * YT * (i + 1)] = jnp.where(ax[i] ^ bx[i], 0.0, rest)
+                masks_of[a * near + k, MASKED:] = rest
             return carry
 
         return one
+
+    def pair_mask(masks_of, pair, c):
+        if c * part < MASKED:
+            return masks_of[pair, c * part : (c + 1) * part]
+        return jnp.concatenate([masks_of[pair, MASKED:]] * (part // (2 * YT)), axis=0)
 
     def weighted(masks_of, cols_of, a, c):
         total = None
         for k in range(near):
-            mask = masks_of[a * near + k, c * part : (c + 1) * part]
+            mask = pair_mask(masks_of, a * near + k, c)
             term = mask * pieces[c][cols_of[a * near + k]].astype(jnp.float32)
             total = term if total is None else total + term
         return total
@@ -292,10 +301,10 @@
 
         @pl.when(helps)
         def _():
-            lax.fori_loop(0, fns, one_far, 0)
+            lax.fori_loop(0, fns, one_far, 0, unroll=4)
             to_helped(c).start()
 
-        lax.fori_loop(0, fns, one, 0)
+        lax.fori_loop(0, fns, one, 0, unroll=4)
 
     half = fns // 2
     lax.fori_loop(0, half, make_masks(False), 0)
@@ -432,7 +441,7 @@
         + [
             pltpu.VMEM((fns * ROWS, LANES), jnp.float32),
             pltpu.VMEM((ROWS, fns, LANES), jnp.float32),
-            pltpu.VMEM((fns * near, ROWS, LANES), jnp.float32),
+            pltpu.VMEM((fns * near, MASKED + 2 * YT, LANES), jnp.float32),
             pltpu.SMEM(conf.shape, jnp.float32),
             pltpu.SMEM(shift_energy.shape, jnp.float32),
             pltpu.SMEM(kern.shape, jnp.float32),
@@ -443,7 +452,7 @@
             pltpu.VMEM(kern.shape, jnp.float32),
             pltpu.SMEM(margins.shape, jnp.int32),
             pltpu.SMEM(kern.shape, jnp.float32),
-            pltpu.VMEM((fns * near, ROWS, LANES), jnp.float32),
+            pltpu.VMEM((fns * near, MASKED + 2 * YT, LANES), jnp.float32),
             pltpu.SMEM((fns * near,), jnp.int32),
             pltpu.VMEM((CHUNKS, fns, ROWS // CHUNKS, LANES), jnp.bfloat16),
             pltpu.VMEM((CHUNKS, fns, ROWS // CHUNKS, LANES), jnp.bfloat16),

time: 21.8 us -> 20.9 us (0.959)
  Pallas kernels: 21 us -> 20.1 us
    pallas_call x1, Pallas kernels: 19.9 us -> 19 us  [on_device(): pl.pallas_call(functools.partial(gather_kernel, groups, devs), out_shape=...]
where the time goes in v5:
time: 20.9 us; the launch traced here: 20.7 us
  Pallas kernels  20.1 us (96%)
  between operations  0.64 us (3%)
    pallas_call x1, Pallas kernels, on_device(): pl.pallas_call(functools.partial(gather_kernel, groups, devs), out_shape=...  19 us
    pallas_call x1, Pallas kernels, on_device(): pl.pallas_call(step_kernel, out_shape=(jax.ShapeDtypeStruct((fns, cells),...  1.09 us

profile of v5, /device:TPU:0, one launch (start us, length us, event | category | flops | bytes accessed | tf_op | source)
XLA Modules:
  0.0 20.7 jit_solution(15767755085765145917)
XLA Ops:
  0.6 19.0 %shard_map.77 = (f32[512,128]{1,0:T(8,128)S(1)}, s32[3,8,128]{2,1,0:T(8,128)S(1)}, bf16[8,8192]{1,0:T(8,128)(2,1)S(1)}) custom-call(bf16[8,8192]{1,0:T(8,128)(2,1)} %phi_hbm.1, f32[8]{0:T(128)} %conf_hbm.1, f32[8]{0:T(128)} %shift_hbm.1, f32[8,80]{1,0:T(8,128)} %kern_hbm.1, s32[8,8]{1,0:T(8,128)} %margins_hbm.1, s32[3,256]{1,0:T(4,128)} %bitcast.1), custom_call_target="tpu_custom_call" | custom-call | tf_op jit(solution)/shard_map/pallas_call | solution.py:431
  19.7 1.1 %shard_map.78 = (f32[8,8192]{1,0:T(8,128)}, bf16[8,8192]{1,0:T(8,128)(2,1)}) custom-call(f32[512,128]{1,0:T(8,128)S(1)} %get-tuple-element.5.sums_ref, s32[3,8,128]{2,1,0:T(8,128)S(1)} %get-tuple-element.6.off_ref, bf16[8,8192]{1,0:T(8,128)(2,1)S(1)} %get-tuple-element.7.phi_ref), custom_call_target="tpu_custom_call" | custom-call | tf_op jit(solution)/shard_map/pallas_call | solution.py:476

commit v6 on v3

--- a/solution.py
+++ b/solution.py
@@ -15,6 +15,8 @@
 YT = BY // YL
 ROWS = BX * YT
 CHUNKS = 4
+TOP = 8
+MASKED = TOP * YT
 MESH = pl.DeviceIdType.MESH
 
 
@@ -107,30 +109,29 @@
     shape = (fns, LANES)
     lane = lax.broadcasted_iota(jnp.int32, shape, 1)
     yl, zz = lane // BZ, lane % BZ
-    zf = (zz.astype(jnp.float32) - (BZ - 1) / 2.0) / BZ
     zero = jnp.zeros(shape, jnp.float32)
 
     def phi_row(t):
         return phi_ref[:, t * LANES : (t + 1) * LANES].astype(jnp.float32)
 
+    zf = (zz.astype(jnp.float32) - (BZ - 1) / 2.0) / BZ
+    yf = [((yl + t * YL).astype(jnp.float32) - (BY - 1) / 2.0) / BY for t in range(YT)]
+    plane_coef = [conf * (y * y + zf * zf) - shift + 3.0 for y in yf]
+    first_y, last_y, first_z, last_z = yl == 0, yl == YL - 1, zz == 0, zz == BZ - 1
+    before, rows = [zero] * YT, [phi_row(t) for t in range(YT)]
     for x in range(BX):
-        xf = ((x - (BX - 1) / 2.0) / BX) ** 2
-        rows = [phi_row(x * YT + t) for t in range(YT)]
+        after = [phi_row((x + 1) * YT + t) for t in range(YT)] if x < BX - 1 else [zero] * YT
         ups = [pltpu.roll(r, LANES - BZ, 1) for r in rows] + [zero]
         downs = [zero] + [pltpu.roll(r, BZ, 1) for r in rows]
+        x_coef = conf * ((x - (BX - 1) / 2.0) / BX) ** 2
         for t in range(YT):
             field = rows[t]
-            lap = phi_row((x + 1) * YT + t) if x < BX - 1 else zero
-            if x > 0:
-                lap = lap + phi_row((x - 1) * YT + t)
-            lap = lap + jnp.where(yl < YL - 1, ups[t], ups[t + 1])
-            lap = lap + jnp.where(yl > 0, downs[t + 1], downs[t])
-            lap = lap + jnp.where(zz < BZ - 1, pltpu.roll(field, LANES - 1, 1), 0.0)
-            lap = lap + jnp.where(zz > 0, pltpu.roll(field, 1, 1), 0.0)
-            lap = lap - 6.0 * field
-            yf = ((yl + t * YL).astype(jnp.float32) - (BY - 1) / 2.0) / BY
-            radius = xf + yf * yf + zf * zf
-            work[x * YT + t] = -0.5 * lap + conf * radius * field - shift * field
+            near_x = before[t] + after[t]
+            near_y = jnp.where(last_y, ups[t + 1], ups[t]) + jnp.where(first_y, downs[t], downs[t + 1])
+            near_z = jnp.where(last_z, 0.0, pltpu.roll(field, LANES - 1, 1))
+            near_z = near_z + jnp.where(first_z, 0.0, pltpu.roll(field, 1, 1))
+            work[x * YT + t] = (plane_coef[t] + x_coef) * field - 0.5 * (near_x + near_y + near_z)
+        before, rows = rows, after
 
     def put_flat(t, value):
         flat[pl.ds(t, fns, stride=ROWS), :] = value
@@ -189,27 +190,37 @@
     for copy in copies[4:]:
         copy.wait()
 
-    row = lax.broadcasted_iota(jnp.int32, (ROWS, LANES), 0)
-    lan = lax.broadcasted_iota(jnp.int32, (ROWS, LANES), 1)
-    cell = (row // YT, row % YT * YL + lan // BZ, lan % BZ)
+    sub = lax.broadcasted_iota(jnp.int32, (2 * YT, LANES), 0)
+    lan = lax.broadcasted_iota(jnp.int32, (2 * YT, LANES), 1)
+    y_cell, z_cell = sub % YT * YL + lan // BZ, lan % BZ
+    x_cells = [sub // YT + 2 * i for i in range(TOP // 2)]
+    group_first = gi * per_group
+
+    def sides(at):
+        ox, oy, oz = (offsets_ref[axis, at] for axis in range(3))
+        return [x < ox for x in x_cells], y_cell < oy, z_cell < oz
 
     def make_masks(a, carry):
+        ax, ay, az = sides(base + a)
         for k in range(near):
             b = margins_ref[a, k]
-            gb = b // per_group
-            col = jnp.where(
-                gb == gi,
-                b - gb * per_group,
-                jnp.where(gb == gi - 1, per_group, per_group + fns) + b % fns,
-            )
+            col = b - group_first
+            inside = (col >= 0) & (col < per_group)
+            beyond = jnp.where(col < 0, per_group, per_group + fns) + lax.rem(b, fns)
+            col = jnp.where(inside, col, beyond)
             cols[a * near + k] = col
-            keep = None
-            for axis in range(3):
-                oa, ob = offsets_ref[axis, base + a], offsets_ref[axis, b]
-                out = (cell[axis] < jnp.minimum(oa, ob)) | (cell[axis] >= jnp.maximum(oa, ob))
-                keep = out if keep is None else keep & out
-            masks[a * near + k] = jnp.where(keep, kern_ref[a, col], 0.0)
+            weight = kern_ref[a, col]
+            bx, by, bz = sides(b)
+            rest = jnp.where((ay ^ by) | (az ^ bz), 0.0, weight)
+            for i in range(TOP // 2):
+                masks[a * near + k, 2 * YT * i : 2 * YT * (i + 1)] = jnp.where(ax[i] ^ bx[i], 0.0, rest)
+            masks[a * near + k, MASKED:] = rest
         return carry
+
+    def pair_mask(masks_of, pair, c):
+        if c * part < MASKED:
+            return masks_of[pair, c * part : (c + 1) * part]
+        return jnp.concatenate([masks_of[pair, MASKED:]] * (part // (2 * YT)), axis=0)
 
     def add_up(c):
         for block in range(nz):
@@ -226,13 +237,13 @@
         def one(a, carry):
             total = None
             for k in range(near):
-                mask = masks[a * near + k, c * part : (c + 1) * part]
+                mask = pair_mask(masks, a * near + k, c)
                 term = mask * pieces[c][cols[a * near + k]].astype(jnp.float32)
                 total = term if total is None else total + term
             sums_ref[pl.ds(pl.multiple_of(a * ROWS + c * part, part), part), :] = total
             return carry
 
-        lax.fori_loop(0, fns, one, 0)
+        lax.fori_loop(0, fns, one, 0, unroll=4)
 
     half = fns // 2
     lax.fori_loop(0, half, make_masks, 0)
@@ -331,7 +342,7 @@
         + [
             pltpu.VMEM((fns * ROWS, LANES), jnp.float32),
             pltpu.VMEM((ROWS, fns, LANES), jnp.float32),
-            pltpu.VMEM((fns * near, ROWS, LANES), jnp.float32),
+            pltpu.VMEM((fns * near, MASKED + 2 * YT, LANES), jnp.float32),
             pltpu.SMEM(conf.shape, jnp.float32),
             pltpu.SMEM(shift_energy.shape, jnp.float32),
             pltpu.SMEM(kern.shape, jnp.float32),

time: 19.7 us -> 19.6 us (level)
  no operation moved by 1% of the time
where the time goes in v6:
time: 19.6 us; the launch traced here: 19.4 us
  Pallas kernels  18.8 us (96%)
  between operations  0.64 us (3%)
    pallas_call x1, Pallas kernels, on_device(): pl.pallas_call(functools.partial(gather_kernel, groups, devs), out_shape=...  17.7 us
    pallas_call x1, Pallas kernels, on_device(): pl.pallas_call(step_kernel, out_shape=(jax.ShapeDtypeStruct((fns, cells),...  1.09 us

profile of v6, /device:TPU:0, one launch (start us, length us, event | category | flops | bytes accessed | tf_op | source)
XLA Modules:
  0.0 19.4 jit_solution(17239951774121343238)
XLA Ops:
  0.6 17.7 %shard_map.77 = (f32[512,128]{1,0:T(8,128)S(1)}, s32[3,8,128]{2,1,0:T(8,128)S(1)}, bf16[8,8192]{1,0:T(8,128)(2,1)S(1)}) custom-call(bf16[8,8192]{1,0:T(8,128)(2,1)} %phi_hbm.1, f32[8]{0:T(128)} %conf_hbm.1, f32[8]{0:T(128)} %shift_hbm.1, f32[8,80]{1,0:T(8,128)} %kern_hbm.1, s32[8,8]{1,0:T(8,128)} %margins_hbm.1, s32[3,256]{1,0:T(4,128)} %bitcast.1), custom_call_target="tpu_custom_call" | custom-call | tf_op jit(solution)/shard_map/pallas_call | solution.py:332
  18.3 1.1 %shard_map.78 = (f32[8,8192]{1,0:T(8,128)}, bf16[8,8192]{1,0:T(8,128)(2,1)}) custom-call(f32[512,128]{1,0:T(8,128)S(1)} %get-tuple-element.5.sums_ref, s32[3,8,128]{2,1,0:T(8,128)S(1)} %get-tuple-element.6.off_ref, bf16[8,8192]{1,0:T(8,128)(2,1)S(1)} %get-tuple-element.7.phi_ref), custom_call_target="tpu_custom_call" | custom-call | tf_op jit(solution)/shard_map/pallas_call | solution.py:364
